TPU v7x, 32 devices: a whole 2x2x4 slice. The times are simulated.
32 devices in a mesh: gx: 4 (over y, x), gy: 8 (over z, core).
Axes of the slice: x: 2, y: 2, z: 4, core: 2. Of those that a mesh axis runs over, the one named last changes fastest.
Arguments:
- field: float32 [3, 16, 256, 1024], P(None, None, 'gx', 'gy'), may hold values from -6 to 6
- masks: int32 [2, 7, 8, 32], P(None, None, 'gx', 'gy'), may hold values 0 or 1
Outputs:
- restored: float32 [3, 16, 256, 1024], P(None, None, 'gx', 'gy')
- coarse: float32 [3, 4, 64, 256], replicated
All inputs are finite; a program needn't handle non-finite values. No bound on the sum of `masks` on one device may be relied on, other than what follows from the above.
Results may differ from a plain program's by a relative error of at most 0.00002.
Values sent between devices are 32-bit elements; how exact they have to be, the bound alone decides.
No kernel may reach another device: no remote copies, remote signals or barrier semaphores. Data moves between devices by JAX's collectives and lax.ppermute only.
A program may use at most 128 MiB of HBM per device.

v0:
```python
import functools

import jax
import jax.numpy as jnp
import ml_dtypes
import numpy as np
from jax import lax
from jax.experimental import pallas as pl
from jax.experimental.pallas import tpu as pltpu
from jax.sharding import PartitionSpec as P

F32 = jnp.float32
BF16 = jnp.bfloat16
VMEM_LIMIT = 32 * 1024 * 1024

NV, NZ, NR, NL = 3, 16, 64, 128


def detail_row(k):
    return {2 * k + 1: 1.0, 2 * k: -0.5, 2 * k + 2: -0.5}


def smooth_row(k):
    row = {2 * k: 1.0}
    for j in (k - 1, k):
        for cell, value in detail_row(j).items():
            row[cell] = row.get(cell, 0.0) + 0.25 * value
    return row


def even_row(k):
    return {("s", k): 1.0, ("d", k - 1): -0.25, ("d", k): -0.25}


def odd_row(k):
    row = {("d", k): 1.0}
    for j in (k, k + 1):
        for name, value in even_row(j).items():
            row[name] = row.get(name, 0.0) + 0.5 * value
    return row


def as_bf16(matrix):
    cast = matrix.astype(ml_dtypes.bfloat16)
    assert (cast.astype(np.float64) == matrix).all()
    return cast


def combine(*terms):
    total = {}
    for factor, row in terms:
        for cell, value in row.items():
            total[cell] = total.get(cell, 0.0) + factor * value
    return total


def level_one_columns():
    names = {("s", k): k for k in range(65)}
    names.update({("d", k): 128 + k for k in range(65)})
    names[("d", -1)] = 128 + 65
    return names


def level_two_columns():
    names = {("s", k): k for k in range(33)}
    names.update({("d", k): 64 + k for k in range(33)})
    names[("d", -1)] = 64 + 33
    return names


def smooth_place(k):
    return k + 2


def beyond(n):
    return {"cell": 24 * n, "after": 24 * n + 8, "before": 24 * n + 16}


BEYOND_SMOOTH = {65: 96, 66: 104, -2: 112, -1: 120}


def own_row(kind, k, n):
    place = {name: 128 + lane for name, lane in beyond(n).items()}
    if kind == "d":
        if k == -1:
            return {place["before"]: 1.0, 0: -0.5}
        if k == 64:
            return {place["after"]: 1.0}
        return {(place["cell"] if y == 128 else y): value for y, value in detail_row(k).items()}
    if k in BEYOND_SMOOTH:
        row = {128 + BEYOND_SMOOTH[k]: 1.0}
        return combine((1.0, row), (1.0, {0: -0.125})) if k == -1 else row
    even = place["cell"] if k == 64 else 2 * k
    return combine((1.0, {even: 1.0}), (0.25, own_row("d", k - 1, n)), (0.25, own_row("d", k, n)))


def group_start(n):
    return 16 * (24 * n // 16)


@functools.lru_cache(maxsize=None)
def weights():
    w = {}
    names = level_one_columns()
    forward = np.zeros((4, 256, 256))
    inverse = np.zeros((256, 128))
    for (kind, k), column in names.items():
        for n in range(4):
            for place, value in own_row(kind, k, n).items():
                forward[n, place, column] += value
    for k in range(64):
        for y, row in ((2 * k, even_row(k)), (2 * k + 1, odd_row(k))):
            for name, value in row.items():
                inverse[names[name], y] += value
    short = np.zeros((4, 160, 256))
    for n in range(4):
        at = 128 + group_start(n)
        short[n, :128], short[n, 128:] = forward[n, :128], forward[n, at : at + 32]
        assert abs(short[n]).sum() == abs(forward[n]).sum()
    smooth = np.zeros((256, 128))
    for k in range(-2, 67):
        for place, value in own_row("s", k, 0).items():
            smooth[place, smooth_place(k)] += value
    names2 = level_two_columns()
    forward2 = np.zeros((128, 128))
    inverse2 = np.zeros((128, 128))
    for (kind, k), column in names2.items():
        for cell, value in (smooth_row(k) if kind == "s" else detail_row(k)).items():
            forward2[smooth_place(cell), column] += value
    for k in range(33):
        rows = [(2 * k, even_row(k))] + ([(2 * k + 1, odd_row(k))] if k < 32 else [])
        for y, row in rows:
            for name, value in row.items():
                inverse2[names2[name], y] += value
    back = np.zeros((256, 128))
    back[:65] = inverse[:65]
    back[128 : 128 + 65] = inverse[:65]
    spread = np.zeros((3, 128, 2, 128))
    for k in range(64):
        spread[0, k, 0, k] = 1
    spread[1, 0, 0, 64] = 1
    spread[2, 63, 0, 65] = 1
    for k in range(32):
        spread[0, 64 + k, 1, k] = 1
        spread[0, 64 + k, 1, 64 + k] = 1
    for base in (0, 64):
        spread[1, 64, 1, base + 32] = 1
        spread[2, 95, 1, base + 33] = 1
    w["wide"] = np.concatenate([short.reshape(640, 256), spread.reshape(384, 256)], 0)
    w["narrow"] = np.concatenate([inverse, smooth, back, forward2, inverse2], 0)
    edge = np.zeros((4, 2, 128, 2, 128))

    def put(n, side, lane, row):
        for z in range(8):
            for y, value in row.items():
                j = y - 120 if y >= 120 else y + 8
                edge[n, :, 16 * z + j, side, lane + z] += value

    part = {127: 1.0, 126: -0.5}
    for n in range(4):
        put(n, 0, beyond(n)["cell"], {0: 1.0})
        put(n, 0, beyond(n)["after"], detail_row(0))
        put(n, 1, beyond(n)["before"], part)
    put(0, 0, BEYOND_SMOOTH[65], smooth_row(1))
    put(0, 0, BEYOND_SMOOTH[66], smooth_row(2))
    put(0, 1, BEYOND_SMOOTH[-2], smooth_row(62))
    put(0, 1, BEYOND_SMOOTH[-1], combine((1.0, {126: 1.0}), (0.25, detail_row(62)), (0.25, part)))
    w["edge"] = edge.reshape(1024, 256)
    expand = np.zeros((2, 4, 128))
    for j in range(4):
        expand[0, j, 16 * j : 16 * j + 16] = 1
        expand[1, j, 64 + 8 * j : 64 + 8 * j + 8] = 1
    twice = combine(*[(value, smooth_row(k)) for k, value in smooth_row(0).items()])
    columns = np.zeros((2, 128, 128))
    for m in range(-1, 34):
        for t, value in twice.items():
            if 0 <= 4 * m + t < NL:
                columns[:, 4 * m + t, m + 1] = value
    rows = np.zeros((4, 32, 2, 64))
    for z in range(4):
        places = {m: m for m in range(16)}
        places.update({16: 16 + 2 * z, 17: 17 + 2 * z, -1: 16 + 15 - z})
        for m, place in places.items():
            for t, value in twice.items():
                if 0 <= 4 * m + t < NR:
                    rows[z, place, :, 4 * m + t] = value
    pad = np.zeros((8, 128))
    w["first"] = np.concatenate([columns.reshape(256, 128), rows.reshape(128, 128), expand.reshape(8, 128), pad], 0)
    return {name: as_bf16(matrix) for name, matrix in w.items()}


def two_terms(x):
    high = x.astype(BF16)
    low = (x - high.astype(F32)).astype(BF16)
    return high, low


def dot(a, b):
    return jnp.dot(a, b, preferred_element_type=F32)


def lift_planes(cells):
    half = len(cells) // 2
    even, odd = cells[0::2], cells[1::2]
    detail = [odd[k] - 0.5 * (even[k] + even[min(k + 1, half - 1)]) for k in range(half)]
    smooth = [even[k] + 0.25 * (detail[max(k - 1, 0)] + detail[k]) for k in range(half)]
    return smooth, detail


def unlift_planes(smooth, detail):
    half = len(smooth)
    even = [smooth[k] - 0.25 * (detail[max(k - 1, 0)] + detail[k]) for k in range(half)]
    out = []
    for k in range(half):
        out += [even[k], detail[k] + 0.5 * (even[k] + even[min(k + 1, half - 1)])]
    return out


def lift_rows(load, start):
    even, odd, after = load(start), load(start + 1), load(start + 2)
    before, odd_before = load(start - 2), load(start - 1)
    detail = odd - 0.5 * (even + after)
    detail_before = odd_before - 0.5 * (before + even)
    return even + 0.25 * (detail_before + detail), detail


def unlift_rows(smooth, detail, row):
    here, after = detail(row), detail(row + 1)
    even = smooth(row) - 0.25 * (detail(row - 1) + here)
    next_even = smooth(row + 1) - 0.25 * (here + after)
    return even, here + 0.5 * (even + next_even)


PITCH = 80


def first_kernel(
    field, masks_hbm, table_hbm, lifted, up, down, own_masks, share, cells, twice, masks, table, sems
):
    copies = []
    for v in range(NV):
        for h in range(2):
            part = pl.ds(8 * h, 8)
            copies.append(pltpu.make_async_copy(field.at[v, part], cells.at[v, part], sems.at[2 * v + h]))
    copies.append(pltpu.make_async_copy(masks_hbm, masks, sems.at[2 * NV]))
    copies.append(pltpu.make_async_copy(table_hbm, table, sems.at[2 * NV + 1]))
    for copy in copies:
        copy.start()
    for p in range(NV * NZ):
        lifted[p * PITCH : p * PITCH + 8, :] = jnp.zeros((8, NL), F32)
        lifted[p * PITCH + 72 : p * PITCH + 80, :] = jnp.zeros((8, NL), F32)

    for v in range(NV):
        for copy in copies[2 * v : 2 * v + 2]:
            copy.wait()

        def planes(t, _):
            at = pl.multiple_of(t * 8, 8)
            smooth, detail = lift_planes([cells[v, z, pl.ds(at, 8), :] for z in range(NZ)])
            for k, tile in enumerate(smooth + detail):
                lifted[pl.ds((v * NZ + k) * PITCH + 8 + at, 8), :] = tile
            for k, tile in enumerate(lift_planes(smooth)[0]):
                twice[v * 4 + k, pl.ds(at, 8), :] = tile
            return 0

        lax.fori_loop(0, 8, planes, 0)
        for bz in range(2):

            def row(x):
                return lifted[pl.ds((v * NZ + bz * 8) * PITCH + 8 + x, 8, stride=PITCH), :]

            x = [row(j) for j in range(7 if bz == 0 else 3)]
            first = x[1] - 0.5 * (x[0] + x[2])
            up[v * 6 + bz] = x[0]
            up[v * 6 + 2 + bz] = first
            y = {j: row(j) for j in (range(58, 64) if bz == 0 else (62, 63))}
            part = y[63] - 0.5 * y[62]
            down[v * 4 + bz] = part
            if bz == 0:
                second = x[3] - 0.5 * (x[2] + x[4])
                third = x[5] - 0.5 * (x[4] + x[6])
                up[v * 6 + 4] = x[2] + 0.25 * (first + second)
                up[v * 6 + 5] = x[4] + 0.25 * (second + third)
                before = y[59] - 0.5 * (y[58] + y[60])
                last = y[61] - 0.5 * (y[60] + y[62])
                down[v * 4 + 2] = y[60] + 0.25 * (before + last)
                down[v * 4 + 3] = y[62] + 0.25 * (last + part)

    for copy in copies[2 * NV :]:
        copy.wait()
    for i, out, tile in ((0, up, 18), (1, down, 12)):
        total = jnp.zeros((7, NL), F32)
        for l in range(2):
            flags = masks[l, i].astype(F32).astype(BF16)
            spread = table[384 + 4 * l : 388 + 4 * l, :]
            total += lax.dot_general(flags, spread, (((0,), (0,)), ((), ())), preferred_element_type=F32)
        own_masks[i] = jnp.concatenate([total, jnp.zeros((1, NL), F32)], 0)
        out[tile] = own_masks[i]
    total = jnp.zeros((80, NL), F32)
    for v in range(NV):
        main, extra = [], jnp.zeros((16, NL), F32)
        for z in range(4):
            terms = jnp.concatenate(two_terms(twice[v * 4 + z]), 0)
            part = dot(table[256 + 32 * z : 288 + 32 * z, :], terms)
            main.append(part[:16])
            extra += part[16:]
        terms = jnp.concatenate(two_terms(jnp.concatenate(main + [extra], 0)), 1)
        part = dot(terms, table[0:256, :])
        total += pltpu.roll(part, 35 * v, 1) if v else part
    share[...] = total


def in_hbm(x):
    return pltpu.with_memory_space_constraint(x, pltpu.HBM)


def first_step(field, masks):
    vmem = pl.BlockSpec(memory_space=pltpu.VMEM)
    shapes = [(NV * NZ * PITCH, NL), (19, 8, NL), (13, 8, NL), (2, 8, NL), (80, NL)]
    return pl.pallas_call(
        first_kernel,
        out_shape=[jax.ShapeDtypeStruct(s, F32) for s in shapes],
        in_specs=[pl.BlockSpec(memory_space=pltpu.HBM)] * 3,
        out_specs=[vmem] * 5,
        scratch_shapes=[
            pltpu.VMEM((NV, NZ, NR, NL), F32),
            pltpu.VMEM((NV * 4, NR, NL), F32),
            pltpu.VMEM((2, 2, 4, 7), jnp.int32),
            pltpu.VMEM((400, NL), BF16),
            pltpu.SemaphoreType.DMA((2 * NV + 2,)),
        ],
        compiler_params=pltpu.CompilerParams(vmem_limit_bytes=VMEM_LIMIT),
    )(*[in_hbm(x) for x in (field, masks.transpose(0, 2, 3, 1), jnp.asarray(weights()["first"]))])


ROWS = 40


def edge_kernel(lifted, north, south, own_masks, table, parts, to_left, to_right, packed):
    def lift(step, _):
        v, bz = step // 2, lax.rem(step, 2)
        for z in range(8):
            start = pl.multiple_of((step * 8 + z) * PITCH, 8)
            for t in range(4):
                pair = lift_rows(lambda s: lifted[pl.ds(start + 16 * t + s, 8, stride=2), :], 8)
                for bx in range(2):
                    plane = (2 * bz + bx) * 24 + v * 8 + z
                    parts[pl.ds(pl.multiple_of(plane * ROWS + 8 * t, 8), 8), :] = pair[bx]
        return 0

    lax.fori_loop(0, NV * 2, lift, 0)
    for p in range(4 * NV * 8):
        parts[p * ROWS + 32 : p * ROWS + 40, :] = jnp.zeros((8, NL), F32)
    for v in range(NV):
        for bz in range(2):

            def cell(x):
                return lifted[pl.ds((v * NZ + bz * 8) * PITCH + 8 + x, 8, stride=PITCH), :]

            def at(bx, r):
                return pl.ds(((2 * bz + bx) * 24 + v * 8) * ROWS + r, 8, stride=ROWS)

            before, after, detail = north[v * 4 + bz], south[v * 6 + bz], south[v * 6 + 2 + bz]
            start = cell(0)
            last = cell(63) - 0.5 * (cell(62) + after)
            parts[at(0, 0), :] = parts[at(0, 0), :] + 0.25 * before
            parts[at(0, 31), :] = parts[at(0, 31), :] - 0.125 * after
            parts[at(1, 31), :] = parts[at(1, 31), :] - 0.5 * after
            parts[at(0, 32), :] = after + 0.25 * (last + detail)
            parts[at(1, 32), :] = detail
            parts[at(1, 39), :] = before - 0.5 * start
            if bz == 0:
                parts[at(0, 33), :] = south[v * 6 + 4]
                parts[at(0, 34), :] = south[v * 6 + 5]
                parts[at(0, 38), :] = north[v * 4 + 2]
                parts[at(0, 39), :] = north[v * 4 + 3] - 0.125 * start

    lane = lax.broadcasted_iota(jnp.int32, (8, NL), 1) // 16

    def pack(step, _):
        for t in range(5):
            tile = jnp.zeros((8, NL), F32)
            for z in range(8):
                x = parts[pl.ds(pl.multiple_of((step * 8 + z) * ROWS + 8 * t, 8), 8), :]
                tile = jnp.where(lane == z, pltpu.roll(x, (8 + 16 * z) % NL, 1), tile)
            packed[pl.ds(pl.multiple_of(step * ROWS + 8 * t, 8), 8), :] = tile
        return 0

    lax.fori_loop(0, 4 * NV, pack, 0)
    terms = []
    for n in range(4):
        terms += list(two_terms(packed[n * 120 : (n + 1) * 120, :]))
    sides = dot(jnp.concatenate(terms, 1), table[...])
    to_left[0:120, :] = sides[:, :NL]
    to_right[0:120, :] = sides[:, NL:]
    for out in (to_left, to_right):
        out[120:128, :] = north[12]
        out[128:136, :] = own_masks[0]
        out[136:144, :] = own_masks[1]
        out[144:152, :] = south[18]


def edge_step(lifted, north, south, own_masks):
    vmem = pl.BlockSpec(memory_space=pltpu.VMEM)
    shapes = [(4 * NV * 8 * ROWS, NL), (152, NL), (152, NL)]
    return pl.pallas_call(
        edge_kernel,
        out_shape=[jax.ShapeDtypeStruct(s, F32) for s in shapes],
        in_specs=[vmem] * 5,
        out_specs=[vmem] * 3,
        scratch_shapes=[pltpu.VMEM((480, NL), F32)],
        compiler_params=pltpu.CompilerParams(vmem_limit_bytes=VMEM_LIMIT),
    )(lifted, north, south, own_masks, weights()["edge"])


def join_kernel(*refs):
    shares, out = refs[:-2], refs[-1]
    for n, piece in enumerate(shares):
        out[80 * n : 80 * (n + 1), :] = piece[...]


def join_step(shares, after):
    vmem = pl.BlockSpec(memory_space=pltpu.VMEM)
    return pl.pallas_call(
        join_kernel,
        out_shape=jax.ShapeDtypeStruct((80 * len(shares), NL), F32),
        in_specs=[vmem] * len(shares) + [pl.BlockSpec(memory_space=pl.ANY)],
        out_specs=vmem,
        compiler_params=pltpu.CompilerParams(vmem_limit_bytes=VMEM_LIMIT),
    )(*shares, after)


def mask_lanes(west, east, own_masks, north_mask, south_mask, wide):
    masks = [jnp.concatenate([ref[120 + 8 * i : 128 + 8 * i, :] for i in range(4)], 0) for ref in (east, west)]
    own = jnp.concatenate([north_mask[0], own_masks[0], own_masks[1], south_mask[0]], 0)
    flags = jnp.concatenate([own] + masks, 1).astype(BF16)
    return dot(flags, wide[640:1024, :])


def sides(west, east, v, at, count):
    rows = pl.ds(pl.multiple_of(v * ROWS + at, 8), count)
    beside = west[rows, :] + east[rows, :]
    tiles = [pltpu.roll(beside, NL - z, 1) if z else beside for z in range(8)]
    return two_terms(jnp.concatenate(tiles, 0))


def operand(parts, n, v, at, count, beside):
    main = two_terms(parts[n, pl.ds(v * 8, 8), pl.ds(at, count), :].reshape(8 * count, NL))
    return [jnp.concatenate(pair, 1) for pair in zip(main, beside)]


def low_kernel(
    parts, west, east, own_masks, north_mask, south_mask, wide, narrow, low_back, gain2, low, second, kept2
):
    smooth_w, forward2, inverse2 = narrow.at[256:512], narrow.at[768:896], narrow.at[896:1024]
    lanes = mask_lanes(west, east, own_masks, north_mask, south_mask, wide)
    lane64 = lax.broadcasted_iota(jnp.int32, (1, NL), 1) < 64
    forward2_f = forward2[...].astype(F32)
    for ib in range(4):
        for n in range(4):
            b = 8 * ib + 4 * (n // 2) + n % 2 - 1
            smooth_two = lanes[b : b + 1, NL:] if n else jnp.ones((1, NL), F32)
            row = jnp.where(lane64, smooth_two, lanes[b + 2 : b + 3, NL:])
            both = dot((forward2_f * row).astype(BF16), inverse2[...]).astype(BF16)
            gain2[ib, n, 0:128, :] = both
            gain2[ib, n, 128:256, :] = both

    def smooth_part(v, _):
        planes = pl.ds(v * 8, 8)
        for at, count in ((0, 16), (16, 16), (32, 8)):
            high, low_term = operand(parts, 0, v, at, count, sides(west, east, v, at, count))
            part = (dot(high, smooth_w[...]) + dot(low_term, smooth_w[...])).reshape(8, count, NL)
            if at < 32:
                low[planes, 8 + at : 8 + at + count, :] = part
                if at == 0:
                    low[planes, 56:64, :] = part[:, 0:8]
            else:
                low[planes, 0:8, :] = part
                low[planes, 40:48, :] = part
                low[planes, 48:56, :] = part
        return 0

    lax.fori_loop(0, NV, smooth_part, 0)

    def rows_two(v, _):
        for t in range(3):
            lifted = [
                lift_rows(lambda s: low[v * 8 + p, pl.ds(16 * t + s, 8, stride=2), :], 8) for p in range(8)
            ]
            for bx in range(2):
                smooth, detail = lift_planes([pair[bx] for pair in lifted])
                for bz, part in ((0, smooth), (1, detail)):
                    for z in range(4):
                        second[2 * bz + bx, t, pl.ds(pl.multiple_of((v * 4 + z) * 8, 8), 8), :] = part[z]
        return 0

    lax.fori_loop(0, NV, rows_two, 0)
    ext_two = lax.broadcasted_iota(jnp.int32, (NV * 4, 8, NL), 1) < 4
    for n in range(4):
        for t in range(3):
            terms = jnp.concatenate(two_terms(second[n, t]), 1)
            if t < 2:
                kept2[n, :, 8 + 8 * t : 16 + 8 * t, :] = dot(terms, gain2[t + 1, n]).reshape(NV * 4, 8, NL)
            else:
                below = dot(terms, gain2[3, n]).reshape(NV * 4, 8, NL)
                above = dot(terms, gain2[0, n]).reshape(NV * 4, 8, NL)
                part = jnp.where(ext_two, below, above)
                kept2[n, :, 0:8, :] = part
                kept2[n, :, 24:32, :] = part

    def back_two(v, _):
        for t in range(3):
            pairs = {}
            for bz in range(2):
                for z in range(4):
                    p = v * 4 + z
                    if t < 2:
                        pairs[bz, z] = unlift_rows(
                            lambda r: kept2[2 * bz, p, pl.ds(r, 8), :],
                            lambda r: kept2[2 * bz + 1, p, pl.ds(r, 8), :],
                            8 + 8 * t,
                        )
                    else:
                        even = kept2[2 * bz, p, 24:32, :] - 0.25 * (
                            kept2[2 * bz + 1, p, 23:31, :] + kept2[2 * bz + 1, p, 24:32, :]
                        )
                        pairs[bz, z] = (even, even)
            for parity in range(2 if t < 2 else 1):
                planes = unlift_planes([pairs[0, z][parity] for z in range(4)], [pairs[1, z][parity] for z in range(4)])
                for z in range(8):
                    low_back[v * 8 + z, pl.ds(16 * t + parity, 8, stride=2), :] = planes[z]
        return 0

    lax.fori_loop(0, NV, back_two, 0)


def high_kernel(
    parts, west, east, own_masks, north_mask, south_mask, wide, narrow, low_back, out, gain, kept, cells, sems
):
    inverse, back = narrow.at[0:256], narrow.at[512:768]
    lanes = mask_lanes(west, east, own_masks, north_mask, south_mask, wide)
    forward_f = [wide[160 * n : 160 * (n + 1), :].astype(F32) for n in range(4)]
    for ib in range(4):
        for n in range(4):
            b = 8 * ib + 4 * (n // 2) + n % 2 - 1
            smooth_one = lanes[b : b + 1, 0:NL] if n else jnp.zeros((1, NL), F32)
            row = jnp.concatenate([smooth_one, lanes[b + 2 : b + 3, 0:NL]], 1)
            both = dot((forward_f[n] * row).astype(BF16), inverse[...]).astype(BF16)
            at = 128 + group_start(n)
            gain[ib, n, 0:128, :] = both[0:128]
            gain[ib, n, 128:256, :] = jnp.zeros((128, NL), BF16)
            gain[ib, n, at : at + 32, :] = both[128:160]

    ext_one = lax.broadcasted_iota(jnp.int32, (8, 8, NL), 1) < 4

    def keep(v, _):
        planes = pl.ds(v * 8, 8)
        for ib in range(3):
            at, count = 16 * ib, 16 if ib < 2 else 8
            beside = sides(west, east, v, at, count)
            for n in range(4):
                high, low_term = operand(parts, n, v, at, count, beside)
                if n == 0:
                    terms = jnp.concatenate(two_terms(low_back[planes, at : at + count, :].reshape(8 * count, NL)), 1)
                    base = dot(terms, back[...])
                if ib < 2:
                    part = dot(high, gain[ib + 1, n]) + dot(low_term, gain[ib + 1, n])
                    if n == 0:
                        part = part + base
                    kept[n, planes, 8 + at : 24 + at, :] = part.reshape(8, count, NL)
                else:
                    below = dot(high, gain[3, n]) + dot(low_term, gain[3, n])
                    above = dot(high, gain[0, n]) + dot(low_term, gain[0, n])
                    if n == 0:
                        below = below + base
                    part = jnp.where(ext_one, below.reshape(8, 8, NL), above.reshape(8, 8, NL))
                    kept[n, planes, 0:8, :] = part
                    kept[n, planes, 40:48, :] = part
        return 0

    def back_one(step, _):
        v, t = step // 4, step % 4
        pairs = {}
        for bz in range(2):
            for z in range(8):
                p = v * 8 + z
                pairs[bz, z] = unlift_rows(
                    lambda r: kept[2 * bz, p, pl.ds(8 * t + r, 8), :],
                    lambda r: kept[2 * bz + 1, p, pl.ds(8 * t + r, 8), :],
                    8,
                )
        for parity in range(2):
            planes = unlift_planes([pairs[0, z][parity] for z in range(8)], [pairs[1, z][parity] for z in range(8)])
            for z in range(NZ):
                cells[v, z, pl.ds(16 * t + parity, 8, stride=2), :] = planes[z]
        return 0

    def one(v, _):
        keep(v, 0)
        lax.fori_loop(v * 4, v * 4 + 4, back_one, 0)
        pltpu.make_async_copy(cells.at[v], out.at[v], sems.at[v]).start()
        return 0

    lax.fori_loop(0, NV, one, 0)
    for v in range(NV):
        pltpu.make_async_copy(cells.at[v], out.at[v], sems.at[v]).wait()


def main_specs():
    vmem = pl.BlockSpec(memory_space=pltpu.VMEM)
    return [
        vmem, vmem, vmem, vmem,
        pl.BlockSpec((1, 8, NL), lambda i: (12, 0, 0)), pl.BlockSpec((1, 8, NL), lambda i: (18, 0, 0)),
        vmem, vmem,
    ]


def low_step(*operands):
    w = weights()
    return pl.pallas_call(
        low_kernel,
        grid=(1,),
        out_shape=jax.ShapeDtypeStruct((NV * 8, 48, NL), F32),
        in_specs=main_specs(),
        out_specs=pl.BlockSpec((NV * 8, 48, NL), lambda i: (0, 0, 0)),
        scratch_shapes=[
            pltpu.VMEM((4, 4, 256, NL), BF16),
            pltpu.VMEM((NV * 8, 64, NL), F32),
            pltpu.VMEM((4, 3, NV * 32, NL), F32),
            pltpu.VMEM((4, NV * 4, 40, NL), F32),
        ],
        compiler_params=pltpu.CompilerParams(vmem_limit_bytes=VMEM_LIMIT),
    )(*operands, w["wide"], w["narrow"])


def high_step(low_back, *operands):
    w = weights()
    return pl.pallas_call(
        high_kernel,
        grid=(1,),
        out_shape=jax.ShapeDtypeStruct((NV, NZ, NR, NL), F32),
        in_specs=main_specs() + [pl.BlockSpec((NV * 8, 48, NL), lambda i: (0, 0, 0))],
        out_specs=pl.BlockSpec(memory_space=pltpu.HBM),
        scratch_shapes=[
            pltpu.VMEM((4, 4, 256, NL), BF16),
            pltpu.VMEM((4, NV * 8, 48, NL), F32),
            pltpu.VMEM((NV, NZ, NR, NL), F32),
            pltpu.SemaphoreType.DMA((NV,)),
        ],
        compiler_params=pltpu.CompilerParams(vmem_limit_bytes=VMEM_LIMIT),
    )(*operands, w["wide"], w["narrow"], low_back)


def rows_kernel(count_x, count_z, *refs):
    shares, out = refs[:count_x], refs[count_x + 1]
    me = lax.axis_index("gx")
    row = lax.broadcasted_iota(jnp.int32, (8, NL), 0)
    for r in range(count_x):
        at = pl.multiple_of(16 * (me ^ r), 16)
        for j in range(count_z):
            for z in range(4):
                out[j, z, pl.ds(at, 16), :] = shares[r][80 * j + 16 * z : 80 * j + 16 * z + 16, :]
    for r in range(count_x):
        i = me ^ r
        below = pl.multiple_of(16 * lax.rem(i + 1, count_x), 16)
        above = pl.multiple_of(16 * lax.rem(i + count_x - 1, count_x) + 8, 8)
        for j in range(count_z):
            low = shares[r][80 * j + 64 : 80 * j + 72, :]
            high = shares[r][80 * j + 72 : 80 * j + 80, :]
            for z in range(4):
                first = pltpu.roll(low, 8 - 2 * z, 0) if z else low
                last = pltpu.roll(high, z, 0) if z else high
                out[j, z, pl.ds(below, 8), :] += jnp.where(row < 2, first, 0.0)
                out[j, z, pl.ds(above, 8), :] += jnp.where(row == 7, last, 0.0)


def rows_step(pieces, count_z, after):
    vmem = pl.BlockSpec(memory_space=pltpu.VMEM)
    count_x = len(pieces)
    return pl.pallas_call(
        functools.partial(rows_kernel, count_x, count_z),
        out_shape=jax.ShapeDtypeStruct((count_z, 4, 16 * count_x, NL), F32),
        in_specs=[vmem] * count_x + [pl.BlockSpec(memory_space=pl.ANY)],
        out_specs=vmem,
        compiler_params=pltpu.CompilerParams(vmem_limit_bytes=VMEM_LIMIT),
    )(*pieces, after)


def coarse_kernel(count_x, count_y, own, other, out_hbm, out, sems):
    me = lax.axis_index("gy")
    me_z, is_even = lax.shift_right_logical(me, 1), lax.rem(me, 2) == 0
    lane = lax.broadcasted_iota(jnp.int32, (8, NL), 1)

    def block(i, _):
        rows = pl.ds(pl.multiple_of(8 * i, 8), 8)
        for z in range(4):
            pieces = []
            for j in range(count_y // 2):
                mine, theirs = own[j ^ me_z, z, rows, :], other[j ^ me_z, z, rows, :]
                pieces += [jnp.where(is_even, mine, theirs), jnp.where(is_even, theirs, mine)]
            for v in range(NV):
                for t in range(count_y // 4):
                    total = jnp.zeros((8, NL), F32)
                    for q in range(-1, 5):
                        start = 32 * q - 1
                        shift = (start - 35 * v) % NL
                        piece = pieces[(4 * t + q) % count_y]
                        turned = pltpu.roll(piece, shift, 1) if shift else piece
                        total += jnp.where((lane >= start) & (lane < start + 35), turned, 0.0)
                    out[v, z, rows, NL * t : NL * (t + 1)] = total
        return 0

    def copy(i):
        rows = pl.ds(pl.multiple_of(16 * i, 16), 16)
        return pltpu.make_async_copy(out.at[:, :, rows], out_hbm.at[:, :, rows], sems.at[i])

    def pair(i, _):
        block(2 * i, 0)
        block(2 * i + 1, 0)
        copy(i).start()
        return 0

    lax.fori_loop(0, count_x, pair, 0)
    for i in range(count_x):
        copy(i).wait()


def coarse_step(own, other, count_x, count_y):
    vmem = pl.BlockSpec(memory_space=pltpu.VMEM)
    shape = (NV, 4, 16 * count_x, 32 * count_y)
    return pl.pallas_call(
        functools.partial(coarse_kernel, count_x, count_y),
        out_shape=jax.ShapeDtypeStruct(shape, F32),
        in_specs=[vmem, vmem],
        out_specs=pl.BlockSpec(memory_space=pltpu.HBM),
        scratch_shapes=[pltpu.VMEM(shape, F32), pltpu.SemaphoreType.DMA((count_x,))],
        compiler_params=pltpu.CompilerParams(vmem_limit_bytes=VMEM_LIMIT),
    )(own, other)


def shifted(x, axis, step):
    count = lax.axis_size(axis)
    return lax.ppermute(x, axis, [(i, (i + step) % count) for i in range(count)])


def swapped(x, axis, distance):
    return lax.ppermute(x, axis, [(i, i ^ distance) for i in range(lax.axis_size(axis))])


def body(field, masks):
    count_x, count_y = lax.axis_size("gx"), lax.axis_size("gy")
    lifted, up, down, own_masks, share = first_step(field, masks)
    south = shifted(up, "gx", -1)
    north = shifted(down, "gx", 1)
    shares = [share] + [swapped(share, "gy", r) for r in range(2, count_y, 2)]
    parts, to_left, to_right = edge_step(lifted, north, south, own_masks)
    west = shifted(to_right, "gy", 1)
    east = shifted(to_left, "gy", -1)
    joined = join_step(shares, to_left)
    pieces = [joined] + [swapped(joined, "gx", r) for r in range(1, count_x)]
    operands = (parts.reshape(4, NV * 8, ROWS, NL), west, east, own_masks, north, south)
    low_back = low_step(*operands)
    own = rows_step(pieces, count_y // 2, low_back)
    other = swapped(own, "gy", 1)
    restored = high_step(low_back, *operands)
    return restored, coarse_step(own, other, count_x, count_y)


def solution(mesh):
    placed = P(None, None, "gx", "gy")
    return jax.shard_map(
        body,
        mesh=mesh,
        in_specs=(placed, placed),
        out_specs=(placed, P()),
        check_vma=False,
    )
```

profile of v0, /device:TPU:0, one launch (start us, length us, event | category | flops | bytes accessed | tf_op | source)
XLA Modules:
  0.0 34.5 jit_solution(2227735117695325368)
XLA Ops:
  0.6 0.0 copy-start.2
  0.6 0.0 copy-start
  0.7 0.0 copy-start.1
  0.7 2.4 %shard_map.77 = (f32[3840,128]{1,0:T(8,128)S(1)}, f32[19,8,128]{2,1,0:T(8,128)S(1)}, f32[13,8,128]{2,1,0:T(8,128)S(1)}, f32[2,8,128]{2,1,0:T(8,128)S(1)}, f32[80,128]{1,0:T(8,128)S(1)}) custom-call(f32[3,16,64,128]{3,2,1,0:T(8,128)} %field.1, s32[2,2,4,7]{3,2,1,0:T(4,128)} %bitcast.4, bf16[400,128]{1,0:T(8,128)(2,1)} %constant.8.clone.table_hbm), custom_call_target="tpu_custom_call" | custom-call | tf_op jit(solution)/shard_map/pallas_call | solution.py:320
  3.1 3.9 %collective-permute-start.1 = (f32[19,8,128]{2,1,0:T(8,128)S(1)}, f32[19,8,128]{2,1,0:T(8,128)S(1)}, u32[]{:S(2)}, u32[]{:S(2)}) collective-permute-start(f32[19,8,128]{2,1,0:T(8,128)S(1)} %get-tuple-element.12), channel_id=1, source_target_pairs={{0,24},{8,0},{16,8},{24,16},{1,25},{9,1},{17,9},{25,17},{2,26},{10... | collective-permute-start | bytes 233480 | tf_op jit(solution)/shard_map/ppermute | solution.py:743
  7.0 0.0 collective-permute-start
  7.0 1.6 %collective-permute-start.4 = (f32[80,128]{1,0:T(8,128)S(1)}, f32[80,128]{1,0:T(8,128)S(1)}, u32[]{:S(2)}, u32[]{:S(2)}) collective-permute-start(f32[80,128]{1,0:T(8,128)S(1)} %get-tuple-element.17.refs_0_), channel_id=1, source_target_pairs={{0,2},{1,3},{2,0},{3,1},{4,6},{5,7},{6,4},{7,5},{8,10},{9,11},{10,... | collective-permute-start | bytes 122888 | tf_op jit(solution)/shard_map/ppermute | solution.py:747
  8.6 2.6 %collective-permute-start.5 = (f32[80,128]{1,0:T(8,128)S(1)}, f32[80,128]{1,0:T(8,128)S(1)}, u32[]{:S(2)}, u32[]{:S(2)}) collective-permute-start(f32[80,128]{1,0:T(8,128)S(1)} %get-tuple-element.17.refs_0_), channel_id=1, source_target_pairs={{0,4},{1,5},{2,6},{3,7},{4,0},{5,1},{6,2},{7,3},{8,12},{9,13},{10,... | collective-permute-start | bytes 122888 | tf_op jit(solution)/shard_map/ppermute | solution.py:747
  11.2 0.2 collective-permute-start.6
  11.4 0.6 %collective-permute-done.north.north_mask = f32[13,8,128]{2,1,0:T(8,128)S(1)} collective-permute-done((f32[13,8,128]{2,1,0:T(8,128)S(1)}, f32[13,8,128]{2,1,0:T(8,128)S(1)}, u32[]{:S(2)}, u32[]{:S(2)}) %collective-permute-start) | collective-permute-done | bytes 53280 | tf_op jit(solution)/shard_map/ppermute | solution.py:743
  12.0 0.0 collective-permute-done.1.south.south_mask
  12.0 1.9 %shard_map.78 = (f32[3840,128]{1,0:T(8,128)S(1)}, f32[152,128]{1,0:T(8,128)S(1)}, f32[152,128]{1,0:T(8,128)S(1)}) custom-call(f32[3840,128]{1,0:T(8,128)S(1)} %get-tuple-element.10.lifted, f32[13,8,128]{2,1,0:T(8,128)S(1)} %collective-permute-done.north.north_mask, f32[19,8,128]{2,1,0:T(8,128)S(1)} %collective-permute-done.1.south.south_mask, ...), custom_call_target="tpu_custom_call" | custom-call | tf_op jit(solution)/shard_map/pallas_call | solution.py:406
  14.0 0.0 collective-permute-done.4.refs_1_
  14.0 3.0 %collective-permute-done.6.refs_3_ = f32[80,128]{1,0:T(8,128)S(1)} collective-permute-done((f32[80,128]{1,0:T(8,128)S(1)}, f32[80,128]{1,0:T(8,128)S(1)}, u32[]{:S(2)}, u32[]{:S(2)}) %collective-permute-start.6) | collective-permute-done | bytes 40992 | tf_op jit(solution)/shard_map/ppermute | solution.py:747
  17.0 2.0 %collective-permute-start.7 = (f32[320,128]{1,0:T(8,128)S(1)}, f32[320,128]{1,0:T(8,128)S(1)}, u32[]{:S(2)}, u32[]{:S(2)}) collective-permute-start(f32[320,128]{1,0:T(8,128)S(1)} %shard_map.81.refs_0_), channel_id=1, source_target_pairs={{0,8},{8,0},{16,24},{24,16},{1,9},{9,1},{17,25},{25,17},{2,10},{10... | collective-permute-start | bytes 491528 | tf_op jit(solution)/shard_map/ppermute | solution.py:747
  19.0 1.5 %collective-permute-start.8 = (f32[320,128]{1,0:T(8,128)S(1)}, f32[320,128]{1,0:T(8,128)S(1)}, u32[]{:S(2)}, u32[]{:S(2)}) collective-permute-start(f32[320,128]{1,0:T(8,128)S(1)} %shard_map.81.refs_0_), channel_id=1, source_target_pairs={{0,16},{8,24},{16,0},{24,8},{1,17},{9,25},{17,1},{25,9},{2,18},{10... | collective-permute-start | bytes 491528 | tf_op jit(solution)/shard_map/ppermute | solution.py:747
  20.5 0.0 collective-permute-start.9
  20.6 3.5 %collective-permute-start.3 = (f32[152,128]{1,0:T(8,128)S(1)}, f32[152,128]{1,0:T(8,128)S(1)}, u32[]{:S(2)}, u32[]{:S(2)}) collective-permute-start(f32[152,128]{1,0:T(8,128)S(1)} %get-tuple-element.16.refs_4_), channel_id=1, source_target_pairs={{0,7},{1,0},{2,1},{3,2},{4,3},{5,4},{6,5},{7,6},{8,15},{9,8},{10,9... | collective-permute-start | bytes 233480 | tf_op jit(solution)/shard_map/ppermute | solution.py:743
  24.1 2.1 %collective-permute-done.2.west = f32[152,128]{1,0:T(8,128)S(1)} collective-permute-done((f32[152,128]{1,0:T(8,128)S(1)}, f32[152,128]{1,0:T(8,128)S(1)}, u32[]{:S(2)}, u32[]{:S(2)}) %collective-permute-start.2) | collective-permute-done | bytes 77856 | tf_op jit(solution)/shard_map/ppermute | solution.py:743
  26.2 2.0 %shard_map.79.low_back.refs_4_ = f32[24,48,128]{2,1,0:T(8,128)S(1)} custom-call(f32[4,24,40,128]{3,2,1,0:T(8,128)S(1)} %bitcast.2, f32[152,128]{1,0:T(8,128)S(1)} %collective-permute-done.2.west, f32[152,128]{1,0:T(8,128)S(1)} %collective-permute-done.3.east, f32[2,8,128]{2,1,0:T(8,128)S(1)} %get-tuple-element.13.own_masks, ...), custom_call_target="tpu_custom_call" | custom-call | tf_op jit(solution)/shard_map/pallas_call | solution.py:620
  28.3 0.2 shard_map.82.own
  28.4 0.1 collective-permute-start.10
  28.5 4.1 %shard_map.80 = f32[3,16,64,128]{3,2,1,0:T(8,128)} custom-call(f32[4,24,40,128]{3,2,1,0:T(8,128)S(1)} %bitcast.3, f32[152,128]{1,0:T(8,128)S(1)} %collective-permute-done.2.west, f32[152,128]{1,0:T(8,128)S(1)} %collective-permute-done.3.east, f32[2,8,128]{2,1,0:T(8,128)S(1)} %get-tuple-element.13.own_masks, ...), custom_call_target="tpu_custom_call" | custom-call | tf_op jit(solution)/shard_map/pallas_call | solution.py:638
  32.6 1.8 %shard_map.83 = f32[3,4,64,256]{3,2,1,0:T(8,128)} custom-call(f32[4,4,64,128]{3,2,1,0:T(8,128)S(1)} %shard_map.82.own, f32[4,4,64,128]{3,2,1,0:T(8,128)S(1)} %collective-permute-done.10.other), custom_call_target="tpu_custom_call" | custom-call | tf_op jit(solution)/shard_map/pallas_call | solution.py:731
  (11 shorter events, 0.0 us)
Async XLA Ops:
  0.6 11.4 %copy-start.2 = (bf16[1024,256]{1,0:T(8,128)(2,1)S(1)}, bf16[1024,256]{1,0:T(8,128)(2,1)}, u32[]{:S(2)}) copy-start(bf16[1024,256]{1,0:T(8,128)(2,1)} %constant.9.clone.table) | copy-start | bytes 1572868
  0.6 25.5 %copy-start = (bf16[1024,256]{1,0:T(8,128)(2,1)S(1)}, bf16[1024,256]{1,0:T(8,128)(2,1)}, u32[]{:S(2)}) copy-start(bf16[1024,256]{1,0:T(8,128)(2,1)} %constant.10.clone.wide) | copy-start | bytes 1572868
  0.7 25.5 %copy-start.1 = (bf16[1024,128]{1,0:T(8,128)(2,1)S(1)}, bf16[1024,128]{1,0:T(8,128)(2,1)}, u32[]{:S(2)}) copy-start(bf16[1024,128]{1,0:T(8,128)(2,1)} %constant.11.clone.narrow) | copy-start | bytes 786436
  3.1 9.0 %collective-permute-start.1 = (f32[19,8,128]{2,1,0:T(8,128)S(1)}, f32[19,8,128]{2,1,0:T(8,128)S(1)}, u32[]{:S(2)}, u32[]{:S(2)}) collective-permute-start(f32[19,8,128]{2,1,0:T(8,128)S(1)} %get-tuple-element.12), channel_id=1, source_target_pairs={{0,24},{8,0},{16,8},{24,16},{1,25},{9,1},{17,9},{25,17},{2,26},{10... | collective-permute-start | bytes 233480 | tf_op jit(solution)/shard_map/ppermute | solution.py:743
  7.0 5.0 %collective-permute-start = (f32[13,8,128]{2,1,0:T(8,128)S(1)}, f32[13,8,128]{2,1,0:T(8,128)S(1)}, u32[]{:S(2)}, u32[]{:S(2)}) collective-permute-start(f32[13,8,128]{2,1,0:T(8,128)S(1)} %get-tuple-element.11), channel_id=1, source_target_pairs={{0,8},{8,16},{16,24},{24,0},{1,9},{9,17},{17,25},{25,1},{2,10},{10... | collective-permute-start | bytes 159752 | tf_op jit(solution)/shard_map/ppermute | solution.py:743
  7.0 7.0 %collective-permute-start.4 = (f32[80,128]{1,0:T(8,128)S(1)}, f32[80,128]{1,0:T(8,128)S(1)}, u32[]{:S(2)}, u32[]{:S(2)}) collective-permute-start(f32[80,128]{1,0:T(8,128)S(1)} %get-tuple-element.17.refs_0_), channel_id=1, source_target_pairs={{0,2},{1,3},{2,0},{3,1},{4,6},{5,7},{6,4},{7,5},{8,10},{9,11},{10,... | collective-permute-start | bytes 122888 | tf_op jit(solution)/shard_map/ppermute | solution.py:747
  8.6 5.4 %collective-permute-start.5 = (f32[80,128]{1,0:T(8,128)S(1)}, f32[80,128]{1,0:T(8,128)S(1)}, u32[]{:S(2)}, u32[]{:S(2)}) collective-permute-start(f32[80,128]{1,0:T(8,128)S(1)} %get-tuple-element.17.refs_0_), channel_id=1, source_target_pairs={{0,4},{1,5},{2,6},{3,7},{4,0},{5,1},{6,2},{7,3},{8,12},{9,13},{10,... | collective-permute-start | bytes 122888 | tf_op jit(solution)/shard_map/ppermute | solution.py:747
  11.2 5.8 %collective-permute-start.6 = (f32[80,128]{1,0:T(8,128)S(1)}, f32[80,128]{1,0:T(8,128)S(1)}, u32[]{:S(2)}, u32[]{:S(2)}) collective-permute-start(f32[80,128]{1,0:T(8,128)S(1)} %get-tuple-element.17.refs_0_), channel_id=1, source_target_pairs={{0,6},{1,7},{2,4},{3,5},{4,2},{5,3},{6,0},{7,1},{8,14},{9,15},{10,... | collective-permute-start | bytes 122888 | tf_op jit(solution)/shard_map/ppermute | solution.py:747
  17.0 11.2 %collective-permute-start.7 = (f32[320,128]{1,0:T(8,128)S(1)}, f32[320,128]{1,0:T(8,128)S(1)}, u32[]{:S(2)}, u32[]{:S(2)}) collective-permute-start(f32[320,128]{1,0:T(8,128)S(1)} %shard_map.81.refs_0_), channel_id=1, source_target_pairs={{0,8},{8,0},{16,24},{24,16},{1,9},{9,1},{17,25},{25,17},{2,10},{10... | collective-permute-start | bytes 491528 | tf_op jit(solution)/shard_map/ppermute | solution.py:747
  19.0 9.2 %collective-permute-start.8 = (f32[320,128]{1,0:T(8,128)S(1)}, f32[320,128]{1,0:T(8,128)S(1)}, u32[]{:S(2)}, u32[]{:S(2)}) collective-permute-start(f32[320,128]{1,0:T(8,128)S(1)} %shard_map.81.refs_0_), channel_id=1, source_target_pairs={{0,16},{8,24},{16,0},{24,8},{1,17},{9,25},{17,1},{25,9},{2,18},{10... | collective-permute-start | bytes 491528 | tf_op jit(solution)/shard_map/ppermute | solution.py:747
  20.5 7.7 %collective-permute-start.9 = (f32[320,128]{1,0:T(8,128)S(1)}, f32[320,128]{1,0:T(8,128)S(1)}, u32[]{:S(2)}, u32[]{:S(2)}) collective-permute-start(f32[320,128]{1,0:T(8,128)S(1)} %shard_map.81.refs_0_), channel_id=1, source_target_pairs={{0,24},{8,16},{16,8},{24,0},{1,25},{9,17},{17,9},{25,1},{2,26},{10... | collective-permute-start | bytes 491528 | tf_op jit(solution)/shard_map/ppermute | solution.py:747
  20.6 5.6 %collective-permute-start.2 = (f32[152,128]{1,0:T(8,128)S(1)}, f32[152,128]{1,0:T(8,128)S(1)}, u32[]{:S(2)}, u32[]{:S(2)}) collective-permute-start(f32[152,128]{1,0:T(8,128)S(1)} %get-tuple-element.15), channel_id=1, source_target_pairs={{0,1},{1,2},{2,3},{3,4},{4,5},{5,6},{6,7},{7,0},{8,9},{9,10},{10,1... | collective-permute-start | bytes 233480 | tf_op jit(solution)/shard_map/ppermute | solution.py:743
  20.6 5.6 %collective-permute-start.3 = (f32[152,128]{1,0:T(8,128)S(1)}, f32[152,128]{1,0:T(8,128)S(1)}, u32[]{:S(2)}, u32[]{:S(2)}) collective-permute-start(f32[152,128]{1,0:T(8,128)S(1)} %get-tuple-element.16.refs_4_), channel_id=1, source_target_pairs={{0,7},{1,0},{2,1},{3,2},{4,3},{5,4},{6,5},{7,6},{8,15},{9,8},{10,9... | collective-permute-start | bytes 233480 | tf_op jit(solution)/shard_map/ppermute | solution.py:743
  28.4 4.2 %collective-permute-start.10 = (f32[4,4,64,128]{3,2,1,0:T(8,128)S(1)}, f32[4,4,64,128]{3,2,1,0:T(8,128)S(1)}, u32[]{:S(2)}, u32[]{:S(2)}) collective-permute-start(f32[4,4,64,128]{3,2,1,0:T(8,128)S(1)} %shard_map.82.own), channel_id=1, source_target_pairs={{0,1},{1,0},{2,3},{3,2},{4,5},{5,4},{6,7},{7,6},{8,9},{9,8},{10,11... | collective-permute-start | bytes 1572872 | tf_op jit(solution)/shard_map/ppermute | solution.py:747
where the time goes:
time: 34.7 us; the launch traced here: 34.5 us
  starting transfers between devices  15.5 us (45%)
  Pallas kernels  12.5 us (36%)
  waiting for transfers between devices  5.71 us (16%)
  between operations  0.76 us (2%)
    ppermute x7, starting transfers between devices, swapped(): lax.ppermute(x, axis, [(i, i ^ distance) for i in range(lax.axis_size(axi...  8.03 us
    ppermute x4, starting transfers between devices, shifted(): lax.ppermute(x, axis, [(i, (i + step) % count) for i in range(count)])  7.49 us
    pallas_call x1, Pallas kernels, high_step(): pl.pallas_call(high_kernel, grid=(1,), out_shape=jax.ShapeDtypeStruct((NV...  4.1 us
    ppermute x7, waiting for transfers between devices, swapped(): lax.ppermute(x, axis, [(i, i ^ distance) for i in range(lax.axis_size(axi...  2.98 us
    ppermute x4, waiting for transfers between devices, shifted(): lax.ppermute(x, axis, [(i, (i + step) % count) for i in range(count)])  2.72 us
    pallas_call x1, Pallas kernels, first_step(): pl.pallas_call(first_kernel, out_shape=[jax.ShapeDtypeStruct(s, F32) for...  2.38 us
    pallas_call x1, Pallas kernels, low_step(): pl.pallas_call(low_kernel, grid=(1,), out_shape=jax.ShapeDtypeStruct((NV...  2.02 us
    pallas_call x1, Pallas kernels, edge_step(): pl.pallas_call(edge_kernel, out_shape=[jax.ShapeDtypeStruct(s, F32) for s...  1.94 us
  transfers between devices with their start and end apart: 11, of which 3 were waited for; matrix products, arithmetic and copies ran while one was open for 0% of the time, Pallas kernels for 23%

commit v1 on v0

--- a/solution.py
+++ b/solution.py
@@ -92,10 +92,6 @@
         return combine((1.0, row), (1.0, {0: -0.125})) if k == -1 else row
     even = place["cell"] if k == 64 else 2 * k
     return combine((1.0, {even: 1.0}), (0.25, own_row("d", k - 1, n)), (0.25, own_row("d", k, n)))
-
-
-def group_start(n):
-    return 16 * (24 * n // 16)
 
 
 @functools.lru_cache(maxsize=None)
@@ -112,11 +108,10 @@
         for y, row in ((2 * k, even_row(k)), (2 * k + 1, odd_row(k))):
             for name, value in row.items():
                 inverse[names[name], y] += value
-    short = np.zeros((4, 160, 256))
-    for n in range(4):
-        at = 128 + group_start(n)
-        short[n, :128], short[n, 128:] = forward[n, :128], forward[n, at : at + 32]
-        assert abs(short[n]).sum() == abs(forward[n]).sum()
+    short = np.zeros((144, 256))
+    short[:128] = forward[0, :128]
+    for i, lane in enumerate(beyond(0).values()):
+        short[128 + i] = forward[0, 128 + lane]
     smooth = np.zeros((256, 128))
     for k in range(-2, 67):
         for place, value in own_row("s", k, 0).items():
@@ -146,7 +141,7 @@
     for base in (0, 64):
         spread[1, 64, 1, base + 32] = 1
         spread[2, 95, 1, base + 33] = 1
-    w["wide"] = np.concatenate([short.reshape(640, 256), spread.reshape(384, 256)], 0)
+    w["wide"] = np.concatenate([short, spread.reshape(384, 256)], 0)
     w["narrow"] = np.concatenate([inverse, smooth, back, forward2, inverse2], 0)
     edge = np.zeros((4, 2, 128, 2, 128))
 
@@ -336,7 +331,7 @@
 ROWS = 40
 
 
-def edge_kernel(lifted, north, south, own_masks, table, parts, to_left, to_right, packed):
+def lift_kernel(lifted, parts):
     def lift(step, _):
         v, bz = step // 2, lax.rem(step, 2)
         for z in range(8):
@@ -349,6 +344,25 @@
         return 0
 
     lax.fori_loop(0, NV * 2, lift, 0)
+
+
+def lift_step(lifted):
+    vmem = pl.BlockSpec(memory_space=pltpu.VMEM)
+    return pl.pallas_call(
+        lift_kernel,
+        out_shape=jax.ShapeDtypeStruct((4 * NV * 8 * ROWS, NL), F32),
+        in_specs=[vmem],
+        out_specs=vmem,
+        cost_estimate=pl.CostEstimate(flops=2 * 10**9, bytes_accessed=4 * 10**6, transcendentals=0),
+        compiler_params=pltpu.CompilerParams(vmem_limit_bytes=VMEM_LIMIT),
+    )(lifted)
+
+
+def edge_kernel(parts_in, lifted, north, south, own_masks, table, *rest):
+    count = len(rest) - 5
+    shares, (parts, to_left, to_right, joined, packed) = rest[:count], rest[count:]
+    for n, piece in enumerate(shares):
+        joined[80 * n : 80 * (n + 1), :] = piece[...]
     for p in range(4 * NV * 8):
         parts[p * ROWS + 32 : p * ROWS + 40, :] = jnp.zeros((8, NL), F32)
     for v in range(NV):
@@ -400,41 +414,25 @@
         out[144:152, :] = south[18]
 
 
-def edge_step(lifted, north, south, own_masks):
+def edge_step(parts, lifted, north, south, own_masks, shares):
     vmem = pl.BlockSpec(memory_space=pltpu.VMEM)
-    shapes = [(4 * NV * 8 * ROWS, NL), (152, NL), (152, NL)]
+    shapes = [(4 * NV * 8 * ROWS, NL), (152, NL), (152, NL), (80 * len(shares), NL)]
     return pl.pallas_call(
         edge_kernel,
         out_shape=[jax.ShapeDtypeStruct(s, F32) for s in shapes],
-        in_specs=[vmem] * 5,
-        out_specs=[vmem] * 3,
+        in_specs=[vmem] * (6 + len(shares)),
+        out_specs=[vmem] * 4,
+        input_output_aliases={0: 0},
         scratch_shapes=[pltpu.VMEM((480, NL), F32)],
         compiler_params=pltpu.CompilerParams(vmem_limit_bytes=VMEM_LIMIT),
-    )(lifted, north, south, own_masks, weights()["edge"])
-
-
-def join_kernel(*refs):
-    shares, out = refs[:-2], refs[-1]
-    for n, piece in enumerate(shares):
-        out[80 * n : 80 * (n + 1), :] = piece[...]
-
-
-def join_step(shares, after):
-    vmem = pl.BlockSpec(memory_space=pltpu.VMEM)
-    return pl.pallas_call(
-        join_kernel,
-        out_shape=jax.ShapeDtypeStruct((80 * len(shares), NL), F32),
-        in_specs=[vmem] * len(shares) + [pl.BlockSpec(memory_space=pl.ANY)],
-        out_specs=vmem,
-        compiler_params=pltpu.CompilerParams(vmem_limit_bytes=VMEM_LIMIT),
-    )(*shares, after)
+    )(parts, lifted, north, south, own_masks, weights()["edge"], *shares)
 
 
 def mask_lanes(west, east, own_masks, north_mask, south_mask, wide):
     masks = [jnp.concatenate([ref[120 + 8 * i : 128 + 8 * i, :] for i in range(4)], 0) for ref in (east, west)]
     own = jnp.concatenate([north_mask[0], own_masks[0], own_masks[1], south_mask[0]], 0)
     flags = jnp.concatenate([own] + masks, 1).astype(BF16)
-    return dot(flags, wide[640:1024, :])
+    return dot(flags, wide[144:528, :])
 
 
 def sides(west, east, v, at, count):
@@ -495,18 +493,14 @@
         return 0
 
     lax.fori_loop(0, NV, rows_two, 0)
-    ext_two = lax.broadcasted_iota(jnp.int32, (NV * 4, 8, NL), 1) < 4
     for n in range(4):
         for t in range(3):
             terms = jnp.concatenate(two_terms(second[n, t]), 1)
             if t < 2:
                 kept2[n, :, 8 + 8 * t : 16 + 8 * t, :] = dot(terms, gain2[t + 1, n]).reshape(NV * 4, 8, NL)
             else:
-                below = dot(terms, gain2[3, n]).reshape(NV * 4, 8, NL)
-                above = dot(terms, gain2[0, n]).reshape(NV * 4, 8, NL)
-                part = jnp.where(ext_two, below, above)
-                kept2[n, :, 0:8, :] = part
-                kept2[n, :, 24:32, :] = part
+                kept2[n, :, 0:8, :] = dot(terms, gain2[0, n]).reshape(NV * 4, 8, NL)
+                kept2[n, :, 24:32, :] = dot(terms, gain2[3, n]).reshape(NV * 4, 8, NL)
 
     def back_two(v, _):
         for t in range(3):
@@ -535,48 +529,44 @@
 
 
 def high_kernel(
-    parts, west, east, own_masks, north_mask, south_mask, wide, narrow, low_back, out, gain, kept, cells, sems
+    parts, west, east, own_masks, north_mask, south_mask, wide, narrow, low_back, out, gain, gain_beyond, kept, cells, sems
 ):
     inverse, back = narrow.at[0:256], narrow.at[512:768]
     lanes = mask_lanes(west, east, own_masks, north_mask, south_mask, wide)
-    forward_f = [wide[160 * n : 160 * (n + 1), :].astype(F32) for n in range(4)]
+    forward_f = wide[0:144, :].astype(F32)
     for ib in range(4):
         for n in range(4):
             b = 8 * ib + 4 * (n // 2) + n % 2 - 1
             smooth_one = lanes[b : b + 1, 0:NL] if n else jnp.zeros((1, NL), F32)
             row = jnp.concatenate([smooth_one, lanes[b + 2 : b + 3, 0:NL]], 1)
-            both = dot((forward_f[n] * row).astype(BF16), inverse[...]).astype(BF16)
-            at = 128 + group_start(n)
-            gain[ib, n, 0:128, :] = both[0:128]
-            gain[ib, n, 128:256, :] = jnp.zeros((128, NL), BF16)
-            gain[ib, n, at : at + 32, :] = both[128:160]
-
-    ext_one = lax.broadcasted_iota(jnp.int32, (8, 8, NL), 1) < 4
-
-    def keep(v, _):
-        planes = pl.ds(v * 8, 8)
+            both = dot((forward_f * row).astype(BF16), inverse[...])
+            main = both[0:128].astype(BF16)
+            gain[ib, n, 0:128, :] = main
+            gain[ib, n, 128:256, :] = main
+            gain_beyond[ib, n] = both[128:136]
+
+    def keep(n, _):
+        turn = lax.rem(NL - 24 * n, NL)
         for ib in range(3):
             at, count = 16 * ib, 16 if ib < 2 else 8
-            beside = sides(west, east, v, at, count)
-            for n in range(4):
-                high, low_term = operand(parts, n, v, at, count, beside)
-                if n == 0:
-                    terms = jnp.concatenate(two_terms(low_back[planes, at : at + count, :].reshape(8 * count, NL)), 1)
-                    base = dot(terms, back[...])
-                if ib < 2:
-                    part = dot(high, gain[ib + 1, n]) + dot(low_term, gain[ib + 1, n])
-                    if n == 0:
-                        part = part + base
-                    kept[n, planes, 8 + at : 24 + at, :] = part.reshape(8, count, NL)
-                else:
-                    below = dot(high, gain[3, n]) + dot(low_term, gain[3, n])
-                    above = dot(high, gain[0, n]) + dot(low_term, gain[0, n])
-                    if n == 0:
-                        below = below + base
-                    part = jnp.where(ext_one, below.reshape(8, 8, NL), above.reshape(8, 8, NL))
-                    kept[n, planes, 0:8, :] = part
-                    kept[n, planes, 40:48, :] = part
-        return 0
+            terms = jnp.concatenate(two_terms(parts[n, :, at : at + count, :].reshape(24 * count, NL)), 1)
+            for place, first in (((8 + at, ib + 1),) if ib < 2 else ((40, 3), (0, 0))):
+                product = dot(terms, gain[first, n]).reshape(24, count, NL)
+                rows = [gain_beyond[first, n, i : i + 1, :] for i in range(3)]
+                for v in range(NV):
+                    beside = west[v * ROWS + at : v * ROWS + at + count, :] + east[v * ROWS + at : v * ROWS + at + count, :]
+                    beside = pltpu.roll(beside, turn, 1)
+                    for z in range(8):
+                        part = product[v * 8 + z]
+                        for i in range(3):
+                            part += beside[:, 8 * i + z : 8 * i + z + 1] * rows[i]
+                        kept[n, v * 8 + z, place : place + count, :] = part
+        return 0
+
+    lax.fori_loop(0, 4, keep, 0)
+    for at, count in ((0, 16), (16, 16), (32, 8)):
+        terms = jnp.concatenate(two_terms(low_back[:, at : at + count, :].reshape(24 * count, NL)), 1)
+        kept[0, :, 8 + at : 8 + at + count, :] += dot(terms, back[...]).reshape(24, count, NL)
 
     def back_one(step, _):
         v, t = step // 4, step % 4
@@ -596,7 +586,6 @@
         return 0
 
     def one(v, _):
-        keep(v, 0)
         lax.fori_loop(v * 4, v * 4 + 4, back_one, 0)
         pltpu.make_async_copy(cells.at[v], out.at[v], sems.at[v]).start()
         return 0
@@ -629,6 +618,7 @@
             pltpu.VMEM((4, 3, NV * 32, NL), F32),
             pltpu.VMEM((4, NV * 4, 40, NL), F32),
         ],
+        cost_estimate=pl.CostEstimate(flops=4 * 10**9, bytes_accessed=8 * 10**6, transcendentals=0),
         compiler_params=pltpu.CompilerParams(vmem_limit_bytes=VMEM_LIMIT),
     )(*operands, w["wide"], w["narrow"])
 
@@ -643,10 +633,12 @@
         out_specs=pl.BlockSpec(memory_space=pltpu.HBM),
         scratch_shapes=[
             pltpu.VMEM((4, 4, 256, NL), BF16),
+            pltpu.VMEM((4, 4, 8, NL), F32),
             pltpu.VMEM((4, NV * 8, 48, NL), F32),
             pltpu.VMEM((NV, NZ, NR, NL), F32),
             pltpu.SemaphoreType.DMA((NV,)),
         ],
+        cost_estimate=pl.CostEstimate(flops=4 * 10**9, bytes_accessed=8 * 10**6, transcendentals=0),
         compiler_params=pltpu.CompilerParams(vmem_limit_bytes=VMEM_LIMIT),
     )(*operands, w["wide"], w["narrow"], low_back)
 
@@ -699,14 +691,16 @@
                 mine, theirs = own[j ^ me_z, z, rows, :], other[j ^ me_z, z, rows, :]
                 pieces += [jnp.where(is_even, mine, theirs), jnp.where(is_even, theirs, mine)]
             for v in range(NV):
+                turned = []
+                for j, piece in enumerate(pieces):
+                    shift = (32 * j - 1 - 35 * v) % NL
+                    turned.append(pltpu.roll(piece, shift, 1) if shift else piece)
                 for t in range(count_y // 4):
-                    total = jnp.zeros((8, NL), F32)
-                    for q in range(-1, 5):
-                        start = 32 * q - 1
-                        shift = (start - 35 * v) % NL
-                        piece = pieces[(4 * t + q) % count_y]
-                        turned = pltpu.roll(piece, shift, 1) if shift else piece
-                        total += jnp.where((lane >= start) & (lane < start + 35), turned, 0.0)
+                    total = jnp.where(lane < 2, turned[4 * t - 1], 0.0)
+                    total += jnp.where(lane == NL - 1, turned[(4 * t + 4) % count_y], 0.0)
+                    for q in range(4):
+                        inside = (lane >= 32 * q - 1) & (lane < 32 * q + 34)
+                        total += jnp.where(inside, turned[4 * t + q], 0.0)
                     out[v, z, rows, NL * t : NL * (t + 1)] = total
         return 0
 
@@ -753,10 +747,9 @@
     south = shifted(up, "gx", -1)
     north = shifted(down, "gx", 1)
     shares = [share] + [swapped(share, "gy", r) for r in range(2, count_y, 2)]
-    parts, to_left, to_right = edge_step(lifted, north, south, own_masks)
+    parts, to_left, to_right, joined = edge_step(lift_step(lifted), lifted, north, south, own_masks, shares)
     west = shifted(to_right, "gy", 1)
     east = shifted(to_left, "gy", -1)
-    joined = join_step(shares, to_left)
     pieces = [joined] + [swapped(joined, "gx", r) for r in range(1, count_x)]
     operands = (parts.reshape(4, NV * 8, ROWS, NL), west, east, own_masks, north, south)
     low_back = low_step(*operands)

time: 34.7 us -> 39.7 us (1.14)
  Pallas kernels: 12.5 us -> 16.6 us
  starting transfers between devices: 15.5 us -> 16.2 us
    pallas_call x1, Pallas kernels: 4.1 us -> 8.34 us  [high_step(): pl.pallas_call(high_kernel, grid=(1,), out_shape=jax.ShapeDtypeStruct((NV...]
    ppermute x7, starting transfers between devices: 8.03 us -> 9.65 us  [swapped(): lax.ppermute(x, axis, [(i, i ^ distance) for i in range(lax.axis_size(axi...]
    ppermute x7, waiting for transfers between devices: 2.98 us -> 4.24 us  [swapped(): lax.ppermute(x, axis, [(i, i ^ distance) for i in range(lax.axis_size(axi...]
    ppermute x4, starting transfers between devices: 7.49 us -> 6.51 us  [shifted(): lax.ppermute(x, axis, [(i, (i + step) % count) for i in range(count)])]
    ppermute x4, waiting for transfers between devices: 2.72 us -> 1.81 us  [shifted(): lax.ppermute(x, axis, [(i, (i + step) % count) for i in range(count)])]
  transfers between devices with their start and end apart: 11 -> 11, of which waited for: 3 -> 6; matrix products, arithmetic and copies ran while one was open for 0% -> 0% of each run, Pallas kernels for 23% -> 27%
where the time goes in v1:
time: 39.7 us; the launch traced here: 39.6 us
  Pallas kernels  16.6 us (42%)
  starting transfers between devices  16.2 us (41%)
  waiting for transfers between devices  6.05 us (15%)
  between operations  0.73 us (2%)
    ppermute x7, starting transfers between devices, swapped(): lax.ppermute(x, axis, [(i, i ^ distance) for i in range(lax.axis_size(axi...  9.65 us
    pallas_call x1, Pallas kernels, high_step(): pl.pallas_call(high_kernel, grid=(1,), out_shape=jax.ShapeDtypeStruct((NV...  8.34 us
    ppermute x4, starting transfers between devices, shifted(): lax.ppermute(x, axis, [(i, (i + step) % count) for i in range(count)])  6.51 us
    ppermute x7, waiting for transfers between devices, swapped(): lax.ppermute(x, axis, [(i, i ^ distance) for i in range(lax.axis_size(axi...  4.24 us
    pallas_call x1, Pallas kernels, first_step(): pl.pallas_call(first_kernel, out_shape=[jax.ShapeDtypeStruct(s, F32) for...  2.29 us
    pallas_call x1, Pallas kernels, low_step(): pl.pallas_call(low_kernel, grid=(1,), out_shape=jax.ShapeDtypeStruct((NV...  2.03 us
    pallas_call x1, Pallas kernels, coarse_step(): pl.pallas_call(functools.partial(coarse_kernel, count_x, count_y), out_sh...  1.83 us
    ppermute x4, waiting for transfers between devices, shifted(): lax.ppermute(x, axis, [(i, (i + step) % count) for i in range(count)])  1.81 us
  transfers between devices with their start and end apart: 11, of which 6 were waited for; matrix products, arithmetic and copies ran while one was open for 0% of the time, Pallas kernels for 27%

profile of v1, /device:TPU:0, one launch (start us, length us, event | category | flops | bytes accessed | tf_op | source)
XLA Modules:
  0.0 39.6 jit_solution(13181343395655481734)
XLA Ops:
  0.6 2.3 %shard_map.77 = (f32[3840,128]{1,0:T(8,128)S(1)}, f32[19,8,128]{2,1,0:T(8,128)S(1)}, f32[13,8,128]{2,1,0:T(8,128)S(1)}, f32[2,8,128]{2,1,0:T(8,128)S(1)}, f32[80,128]{1,0:T(8,128)S(1)}) custom-call(f32[3,16,64,128]{3,2,1,0:T(8,128)} %field.1, s32[2,2,4,7]{3,2,1,0:T(4,128)} %bitcast.4, bf16[400,128]{1,0:T(8,128)(2,1)} %constant.8.clone.table_hbm), custom_call_target="tpu_custom_call" | custom-call | tf_op jit(solution)/shard_map/pallas_call | solution.py:315
  2.9 5.1 %collective-permute-start.4 = (f32[80,128]{1,0:T(8,128)S(1)}, f32[80,128]{1,0:T(8,128)S(1)}, u32[]{:S(2)}, u32[]{:S(2)}) collective-permute-start(f32[80,128]{1,0:T(8,128)S(1)} %get-tuple-element.15.rest_0_), channel_id=1, source_target_pairs={{0,6},{1,7},{2,4},{3,5},{4,2},{5,3},{6,0},{7,1},{8,14},{9,15},{10,... | collective-permute-start | bytes 122888 | tf_op jit(solution)/shard_map/ppermute | solution.py:741
  8.0 0.0 collective-permute-start.3
  8.0 0.6 %collective-permute-start.2 = (f32[80,128]{1,0:T(8,128)S(1)}, f32[80,128]{1,0:T(8,128)S(1)}, u32[]{:S(2)}, u32[]{:S(2)}) collective-permute-start(f32[80,128]{1,0:T(8,128)S(1)} %get-tuple-element.15.rest_0_), channel_id=1, source_target_pairs={{0,2},{1,3},{2,0},{3,1},{4,6},{5,7},{6,4},{7,5},{8,10},{9,11},{10,... | collective-permute-start | bytes 122888 | tf_op jit(solution)/shard_map/ppermute | solution.py:741
  8.7 1.6 %collective-permute-start = (f32[13,8,128]{2,1,0:T(8,128)S(1)}, f32[13,8,128]{2,1,0:T(8,128)S(1)}, u32[]{:S(2)}, u32[]{:S(2)}) collective-permute-start(f32[13,8,128]{2,1,0:T(8,128)S(1)} %get-tuple-element.12), channel_id=1, source_target_pairs={{0,8},{8,16},{16,24},{24,0},{1,9},{9,17},{17,25},{25,1},{2,10},{10... | collective-permute-start | bytes 159752 | tf_op jit(solution)/shard_map/ppermute | solution.py:737
  10.3 1.3 %collective-permute-start.1 = (f32[19,8,128]{2,1,0:T(8,128)S(1)}, f32[19,8,128]{2,1,0:T(8,128)S(1)}, u32[]{:S(2)}, u32[]{:S(2)}) collective-permute-start(f32[19,8,128]{2,1,0:T(8,128)S(1)} %get-tuple-element.13), channel_id=1, source_target_pairs={{0,24},{8,0},{16,8},{24,16},{1,25},{9,1},{17,9},{25,17},{2,26},{10... | collective-permute-start | bytes 233480 | tf_op jit(solution)/shard_map/ppermute | solution.py:737
  11.6 0.3 shard_map.78.parts_in
  11.9 1.0 %collective-permute-done.3.rest_2_ = f32[80,128]{1,0:T(8,128)S(1)} collective-permute-done((f32[80,128]{1,0:T(8,128)S(1)}, f32[80,128]{1,0:T(8,128)S(1)}, u32[]{:S(2)}, u32[]{:S(2)}) %collective-permute-start.3) | collective-permute-done | bytes 40992 | tf_op jit(solution)/shard_map/ppermute | solution.py:741
  12.9 0.0 collective-permute-done.2.rest_1_
  12.9 1.2 %collective-permute-done.north.north_mask = f32[13,8,128]{2,1,0:T(8,128)S(1)} collective-permute-done((f32[13,8,128]{2,1,0:T(8,128)S(1)}, f32[13,8,128]{2,1,0:T(8,128)S(1)}, u32[]{:S(2)}, u32[]{:S(2)}) %collective-permute-start) | collective-permute-done | bytes 53280 | tf_op jit(solution)/shard_map/ppermute | solution.py:737
  14.1 0.6 %collective-permute-done.1.south.south_mask = f32[19,8,128]{2,1,0:T(8,128)S(1)} collective-permute-done((f32[19,8,128]{2,1,0:T(8,128)S(1)}, f32[19,8,128]{2,1,0:T(8,128)S(1)}, u32[]{:S(2)}, u32[]{:S(2)}) %collective-permute-start.1) | collective-permute-done | bytes 77856 | tf_op jit(solution)/shard_map/ppermute | solution.py:737
  14.8 1.6 %shard_map.79 = (f32[3840,128]{1,0:T(8,128)S(1)}, f32[152,128]{1,0:T(8,128)S(1)}, f32[152,128]{1,0:T(8,128)S(1)}, f32[320,128]{1,0:T(8,128)S(1)}) custom-call(f32[3840,128]{1,0:T(8,128)S(1)} %shard_map.78.parts_in, f32[3840,128]{1,0:T(8,128)S(1)} %get-tuple-element.11.lifted, ...), custom_call_target="tpu_custom_call", output_to_operand_aliasing={{0}: (0, {})} | custom-call | tf_op jit(solution)/shard_map/pallas_call | solution.py:420
  16.4 0.1 collective-permute-start.5
  16.5 3.5 %collective-permute-start.6 = (f32[152,128]{1,0:T(8,128)S(1)}, f32[152,128]{1,0:T(8,128)S(1)}, u32[]{:S(2)}, u32[]{:S(2)}) collective-permute-start(f32[152,128]{1,0:T(8,128)S(1)} %get-tuple-element.18), channel_id=1, source_target_pairs={{0,7},{1,0},{2,1},{3,2},{4,3},{5,4},{6,5},{7,6},{8,15},{9,8},{10,9... | collective-permute-start | bytes 233480 | tf_op jit(solution)/shard_map/ppermute | solution.py:737
  20.0 2.2 %collective-permute-start.9 = (f32[320,128]{1,0:T(8,128)S(1)}, f32[320,128]{1,0:T(8,128)S(1)}, u32[]{:S(2)}, u32[]{:S(2)}) collective-permute-start(f32[320,128]{1,0:T(8,128)S(1)} %get-tuple-element.19.refs_0_), channel_id=1, source_target_pairs={{0,24},{8,16},{16,8},{24,0},{1,25},{9,17},{17,9},{25,1},{2,26},{10... | collective-permute-start | bytes 491528 | tf_op jit(solution)/shard_map/ppermute | solution.py:741
  22.1 1.7 %collective-permute-start.8 = (f32[320,128]{1,0:T(8,128)S(1)}, f32[320,128]{1,0:T(8,128)S(1)}, u32[]{:S(2)}, u32[]{:S(2)}) collective-permute-start(f32[320,128]{1,0:T(8,128)S(1)} %get-tuple-element.19.refs_0_), channel_id=1, source_target_pairs={{0,16},{8,24},{16,0},{24,8},{1,17},{9,25},{17,1},{25,9},{2,18},{10... | collective-permute-start | bytes 491528 | tf_op jit(solution)/shard_map/ppermute | solution.py:741
  23.8 2.0 %shard_map.80.low_back.refs_4_ = f32[24,48,128]{2,1,0:T(8,128)S(1)} custom-call(f32[4,24,40,128]{3,2,1,0:T(8,128)S(1)} %bitcast.2, f32[152,128]{1,0:T(8,128)S(1)} %collective-permute-done.5.west, f32[152,128]{1,0:T(8,128)S(1)} %collective-permute-done.6.east, f32[2,8,128]{2,1,0:T(8,128)S(1)} %get-tuple-element.14.own_masks, ...), custom_call_target="tpu_custom_call" | custom-call | flops 4000000000 | bytes 8000000 | tf_op jit(solution)/shard_map/pallas_call | solution.py:609
  25.9 1.3 %collective-permute-done.9.refs_3_ = f32[320,128]{1,0:T(8,128)S(1)} collective-permute-done((f32[320,128]{1,0:T(8,128)S(1)}, f32[320,128]{1,0:T(8,128)S(1)}, u32[]{:S(2)}, u32[]{:S(2)}) %collective-permute-start.9) | collective-permute-done | bytes 163872 | tf_op jit(solution)/shard_map/ppermute | solution.py:741
  27.2 1.4 %collective-permute-done.8.refs_2_ = f32[320,128]{1,0:T(8,128)S(1)} collective-permute-done((f32[320,128]{1,0:T(8,128)S(1)}, f32[320,128]{1,0:T(8,128)S(1)}, u32[]{:S(2)}, u32[]{:S(2)}) %collective-permute-start.8) | collective-permute-done | bytes 163872 | tf_op jit(solution)/shard_map/ppermute | solution.py:741
  28.6 0.5 %collective-permute-done.7.refs_1_ = f32[320,128]{1,0:T(8,128)S(1)} collective-permute-done((f32[320,128]{1,0:T(8,128)S(1)}, f32[320,128]{1,0:T(8,128)S(1)}, u32[]{:S(2)}, u32[]{:S(2)}) %collective-permute-start.7) | collective-permute-done | bytes 163872 | tf_op jit(solution)/shard_map/ppermute | solution.py:741
  29.1 0.2 shard_map.82.own
  29.3 0.1 collective-permute-start.10
  29.4 8.3 %shard_map.81 = f32[3,16,64,128]{3,2,1,0:T(8,128)} custom-call(f32[4,24,40,128]{3,2,1,0:T(8,128)S(1)} %bitcast.3, f32[152,128]{1,0:T(8,128)S(1)} %collective-permute-done.5.west, f32[152,128]{1,0:T(8,128)S(1)} %collective-permute-done.6.east, f32[2,8,128]{2,1,0:T(8,128)S(1)} %get-tuple-element.14.own_masks, ...), custom_call_target="tpu_custom_call" | custom-call | flops 4000000000 | bytes 8000000 | tf_op jit(solution)/shard_map/pallas_call | solution.py:628
  37.7 1.8 %shard_map.83 = f32[3,4,64,256]{3,2,1,0:T(8,128)} custom-call(f32[4,4,64,128]{3,2,1,0:T(8,128)S(1)} %shard_map.82.own, f32[4,4,64,128]{3,2,1,0:T(8,128)S(1)} %collective-permute-done.10.other), custom_call_target="tpu_custom_call" | custom-call | tf_op jit(solution)/shard_map/pallas_call | solution.py:725
  (11 shorter events, 0.0 us)
Async XLA Ops:
  2.9 9.0 %collective-permute-start.4 = (f32[80,128]{1,0:T(8,128)S(1)}, f32[80,128]{1,0:T(8,128)S(1)}, u32[]{:S(2)}, u32[]{:S(2)}) collective-permute-start(f32[80,128]{1,0:T(8,128)S(1)} %get-tuple-element.15.rest_0_), channel_id=1, source_target_pairs={{0,6},{1,7},{2,4},{3,5},{4,2},{5,3},{6,0},{7,1},{8,14},{9,15},{10,... | collective-permute-start | bytes 122888 | tf_op jit(solution)/shard_map/ppermute | solution.py:741
  8.0 4.9 %collective-permute-start.3 = (f32[80,128]{1,0:T(8,128)S(1)}, f32[80,128]{1,0:T(8,128)S(1)}, u32[]{:S(2)}, u32[]{:S(2)}) collective-permute-start(f32[80,128]{1,0:T(8,128)S(1)} %get-tuple-element.15.rest_0_), channel_id=1, source_target_pairs={{0,4},{1,5},{2,6},{3,7},{4,0},{5,1},{6,2},{7,3},{8,12},{9,13},{10,... | collective-permute-start | bytes 122888 | tf_op jit(solution)/shard_map/ppermute | solution.py:741
  8.0 4.9 %collective-permute-start.2 = (f32[80,128]{1,0:T(8,128)S(1)}, f32[80,128]{1,0:T(8,128)S(1)}, u32[]{:S(2)}, u32[]{:S(2)}) collective-permute-start(f32[80,128]{1,0:T(8,128)S(1)} %get-tuple-element.15.rest_0_), channel_id=1, source_target_pairs={{0,2},{1,3},{2,0},{3,1},{4,6},{5,7},{6,4},{7,5},{8,10},{9,11},{10,... | collective-permute-start | bytes 122888 | tf_op jit(solution)/shard_map/ppermute | solution.py:741
  8.7 5.4 %collective-permute-start = (f32[13,8,128]{2,1,0:T(8,128)S(1)}, f32[13,8,128]{2,1,0:T(8,128)S(1)}, u32[]{:S(2)}, u32[]{:S(2)}) collective-permute-start(f32[13,8,128]{2,1,0:T(8,128)S(1)} %get-tuple-element.12), channel_id=1, source_target_pairs={{0,8},{8,16},{16,24},{24,0},{1,9},{9,17},{17,25},{25,1},{2,10},{10... | collective-permute-start | bytes 159752 | tf_op jit(solution)/shard_map/ppermute | solution.py:737
  10.3 4.4 %collective-permute-start.1 = (f32[19,8,128]{2,1,0:T(8,128)S(1)}, f32[19,8,128]{2,1,0:T(8,128)S(1)}, u32[]{:S(2)}, u32[]{:S(2)}) collective-permute-start(f32[19,8,128]{2,1,0:T(8,128)S(1)} %get-tuple-element.13), channel_id=1, source_target_pairs={{0,24},{8,0},{16,8},{24,16},{1,25},{9,1},{17,9},{25,17},{2,26},{10... | collective-permute-start | bytes 233480 | tf_op jit(solution)/shard_map/ppermute | solution.py:737
  11.6 3.1 %copy-start = (bf16[1024,256]{1,0:T(8,128)(2,1)S(1)}, bf16[1024,256]{1,0:T(8,128)(2,1)}, u32[]{:S(2)}) copy-start(bf16[1024,256]{1,0:T(8,128)(2,1)} %constant.9.clone.table) | copy-start | bytes 1572868
  14.8 9.1 %copy-start.1 = (bf16[528,256]{1,0:T(8,128)(2,1)S(1)}, bf16[528,256]{1,0:T(8,128)(2,1)}, u32[]{:S(2)}) copy-start(bf16[528,256]{1,0:T(8,128)(2,1)} %constant.10.clone.wide) | copy-start | bytes 811012
  14.8 9.1 %copy-start.2 = (bf16[1024,128]{1,0:T(8,128)(2,1)S(1)}, bf16[1024,128]{1,0:T(8,128)(2,1)}, u32[]{:S(2)}) copy-start(bf16[1024,128]{1,0:T(8,128)(2,1)} %constant.11.clone.narrow) | copy-start | bytes 786436
  16.4 7.4 %collective-permute-start.5 = (f32[152,128]{1,0:T(8,128)S(1)}, f32[152,128]{1,0:T(8,128)S(1)}, u32[]{:S(2)}, u32[]{:S(2)}) collective-permute-start(f32[152,128]{1,0:T(8,128)S(1)} %get-tuple-element.17), channel_id=1, source_target_pairs={{0,1},{1,2},{2,3},{3,4},{4,5},{5,6},{6,7},{7,0},{8,9},{9,10},{10,1... | collective-permute-start | bytes 233480 | tf_op jit(solution)/shard_map/ppermute | solution.py:737
  16.5 7.4 %collective-permute-start.6 = (f32[152,128]{1,0:T(8,128)S(1)}, f32[152,128]{1,0:T(8,128)S(1)}, u32[]{:S(2)}, u32[]{:S(2)}) collective-permute-start(f32[152,128]{1,0:T(8,128)S(1)} %get-tuple-element.18), channel_id=1, source_target_pairs={{0,7},{1,0},{2,1},{3,2},{4,3},{5,4},{6,5},{7,6},{8,15},{9,8},{10,9... | collective-permute-start | bytes 233480 | tf_op jit(solution)/shard_map/ppermute | solution.py:737
  20.0 7.2 %collective-permute-start.9 = (f32[320,128]{1,0:T(8,128)S(1)}, f32[320,128]{1,0:T(8,128)S(1)}, u32[]{:S(2)}, u32[]{:S(2)}) collective-permute-start(f32[320,128]{1,0:T(8,128)S(1)} %get-tuple-element.19.refs_0_), channel_id=1, source_target_pairs={{0,24},{8,16},{16,8},{24,0},{1,25},{9,17},{17,9},{25,1},{2,26},{10... | collective-permute-start | bytes 491528 | tf_op jit(solution)/shard_map/ppermute | solution.py:741
  22.1 6.4 %collective-permute-start.8 = (f32[320,128]{1,0:T(8,128)S(1)}, f32[320,128]{1,0:T(8,128)S(1)}, u32[]{:S(2)}, u32[]{:S(2)}) collective-permute-start(f32[320,128]{1,0:T(8,128)S(1)} %get-tuple-element.19.refs_0_), channel_id=1, source_target_pairs={{0,16},{8,24},{16,0},{24,8},{1,17},{9,25},{17,1},{25,9},{2,18},{10... | collective-permute-start | bytes 491528 | tf_op jit(solution)/shard_map/ppermute | solution.py:741
  23.8 5.3 %collective-permute-start.7 = (f32[320,128]{1,0:T(8,128)S(1)}, f32[320,128]{1,0:T(8,128)S(1)}, u32[]{:S(2)}, u32[]{:S(2)}) collective-permute-start(f32[320,128]{1,0:T(8,128)S(1)} %get-tuple-element.19.refs_0_), channel_id=1, source_target_pairs={{0,8},{8,0},{16,24},{24,16},{1,9},{9,1},{17,25},{25,17},{2,10},{10... | collective-permute-start | bytes 491528 | tf_op jit(solution)/shard_map/ppermute | solution.py:741
  29.3 8.4 %collective-permute-start.10 = (f32[4,4,64,128]{3,2,1,0:T(8,128)S(1)}, f32[4,4,64,128]{3,2,1,0:T(8,128)S(1)}, u32[]{:S(2)}, u32[]{:S(2)}) collective-permute-start(f32[4,4,64,128]{3,2,1,0:T(8,128)S(1)} %shard_map.82.own), channel_id=1, source_target_pairs={{0,1},{1,0},{2,3},{3,2},{4,5},{5,4},{6,7},{7,6},{8,9},{9,8},{10,11... | collective-permute-start | bytes 1572872 | tf_op jit(solution)/shard_map/ppermute | solution.py:741
